TPU v7x, 32 devices: a whole 2x2x4 slice. The times are simulated.
32 devices in a mesh: ctx: 16 (over z, x, core), head: 2 (over y).
Axes of the slice: x: 2, y: 2, z: 4, core: 2. Of those that a mesh axis runs over, the one named last changes fastest.
Arguments:
- query: bfloat16 [4096, 32, 128], P('ctx', 'head'), may hold values from -160 to 160
- key: bfloat16 [4096, 8, 128], P('ctx', 'head'), may hold values from -8 to 8
- value: bfloat16 [4096, 8, 128], P('ctx', 'head'), may hold values from -6 to 6
- d_mixed: bfloat16 [4096, 4096], P('ctx', 'head'), may hold values from -6 to 6
- out_weight: bfloat16 [4096, 4096], P('head'), may hold values from -1 to 1
- block_keys: int32 [32, 20], P('ctx'), may hold values from 0 to 31, as said below
- scope_ids: int32 [4096], P('ctx'), may hold values from 0 to 15
Outputs:
- grad_query: bfloat16 [4096, 32, 128], P('ctx', 'head')
- grad_key: bfloat16 [4096, 8, 128], P('ctx', 'head')
- grad_value: bfloat16 [4096, 8, 128], P('ctx', 'head')
Inputs may be any that keep to these rules, and one draw needn't show every extreme that they name: `block_keys`: row b names 20 distinct key blocks, block b itself among them.
All inputs are finite; a program needn't handle non-finite values.
Results may differ from a plain program's by a relative error of at most 0.0059.
Values may be sent and summed in bfloat16 or wider, within the bound.
A program may use at most 192 MiB of HBM per device.

v0:
```python
import math

import jax
import jax.numpy as jnp
from jax import lax
from jax.sharding import PartitionSpec as P

BLK = 128


def score_pair(q_block, scope_q, k_block, scope_k, scale):
    scores = (
        jnp.einsum("ignd,jgd->gnij", q_block, k_block, preferred_element_type=jnp.float32) * scale
    )
    scope_key = scope_k.astype(jnp.float32)
    visible = (scope_key[None, :] == scope_q[:, None]) | (scope_key[None, :] == 0.0)
    return (scores, visible)


def backward_pair(
    q_block, do_block, lse_here, delta_here, scope_q, k_block, v_block, scope_k, scale
):
    scores, visible = score_pair(q_block, scope_q, k_block, scope_k, scale)
    probs = jnp.where(visible, jnp.exp(scores - lse_here[..., None]), 0.0)
    rounded = probs.astype(jnp.bfloat16)
    grad_v = jnp.einsum("gnij,ignd->jgd", rounded, do_block, preferred_element_type=jnp.float32)
    dprobs = jnp.einsum("ignd,jgd->gnij", do_block, v_block, preferred_element_type=jnp.float32)
    dscores = (probs * (dprobs - delta_here[..., None]) * scale).astype(jnp.bfloat16)
    grad_q = jnp.einsum("gnij,jgd->ignd", dscores, k_block, preferred_element_type=jnp.float32)
    grad_k = jnp.einsum("gnij,ignd->jgd", dscores, q_block, preferred_element_type=jnp.float32)
    return (grad_q, grad_k, grad_v)


def on_device(query, key, value, d_mixed, out_weight, block_keys, scope_ids):
    tokens_here = query.shape[0]
    heads_here = query.shape[1]
    width = query.shape[2]
    kv_here = key.shape[1]
    group = heads_here // kv_here
    blocks = tokens_here // BLK
    scale = 1.0 / math.sqrt(width)
    d_out = lax.dot_general(
        lax.all_gather(d_mixed, "head", axis=1, tiled=True),
        out_weight,
        (((1,), (1,)), ((), ())),
        preferred_element_type=jnp.float32,
    ).astype(jnp.bfloat16)
    q_blocks = query.reshape(blocks, BLK, kv_here, group, width)
    do_blocks = d_out.reshape(blocks, BLK, kv_here, group, width)
    own_scope = scope_ids.reshape(blocks, BLK).astype(jnp.float32)
    all_keys, all_values, all_scope = (
        lax.all_gather(key, "ctx", axis=0, tiled=True),
        lax.all_gather(value, "ctx", axis=0, tiled=True),
        lax.all_gather(scope_ids.astype(jnp.bfloat16), "ctx", axis=0, tiled=True),
    )
    total_blocks = all_keys.shape[0] // BLK
    k_all = all_keys.reshape(total_blocks, BLK, kv_here, width)
    v_all = all_values.reshape(total_blocks, BLK, kv_here, width)
    s_all = all_scope.reshape(total_blocks, BLK)
    slots = block_keys.shape[1]
    grad_k_all = jnp.zeros((total_blocks, BLK, kv_here, width), jnp.float32)
    grad_v_all = jnp.zeros((total_blocks, BLK, kv_here, width), jnp.float32)
    grad_rows = []
    for row in range(blocks):
        listed = block_keys[row]
        k_near = k_all[listed].reshape(slots * BLK, kv_here, width)
        v_near = v_all[listed].reshape(slots * BLK, kv_here, width)
        s_near = s_all[listed].reshape(slots * BLK)
        scores, visible = score_pair(q_blocks[row], own_scope[row], k_near, s_near, scale)
        masked = jnp.where(visible, scores, -1e30)
        high = jnp.max(masked, axis=-1)
        total = jnp.sum(jnp.where(visible, jnp.exp(scores - high[..., None]), 0.0), axis=-1)
        lse_here = high + jnp.log(total)
        probs = jnp.where(visible, jnp.exp(scores - lse_here[..., None]), 0.0)
        attn_out = jnp.einsum(
            "gnij,jgd->ignd", probs, v_near.astype(jnp.float32), precision=lax.Precision.HIGHEST
        )
        delta = jnp.sum(do_blocks[row].astype(jnp.float32) * attn_out, axis=-1)
        delta_here = jnp.transpose(delta, (1, 2, 0))
        grad_q, part_k, part_v = backward_pair(
            q_blocks[row],
            do_blocks[row],
            lse_here,
            delta_here,
            own_scope[row],
            k_near,
            v_near,
            s_near,
            scale,
        )
        grad_rows.append(grad_q)
        grad_k_all = grad_k_all.at[listed].add(part_k.reshape(slots, BLK, kv_here, width))
        grad_v_all = grad_v_all.at[listed].add(part_v.reshape(slots, BLK, kv_here, width))
    combined = jnp.concatenate([grad_k_all, grad_v_all], axis=-1).reshape(
        total_blocks * BLK, kv_here, 2 * width
    )
    home = lax.psum_scatter(combined, "ctx", scatter_dimension=0, tiled=True)
    grad_query = jnp.stack(grad_rows).reshape(tokens_here, heads_here, width).astype(jnp.bfloat16)
    grad_key = home[:, :, :width].astype(jnp.bfloat16)
    grad_value = home[:, :, width:].astype(jnp.bfloat16)
    return (grad_query, grad_key, grad_value)


def solution(mesh):
    in_specs = (
        P("ctx", "head", None),
        P("ctx", "head", None),
        P("ctx", "head", None),
        P("ctx", "head"),
        P("head", None),
        P("ctx", None),
        P("ctx"),
    )
    out_specs = (P("ctx", "head", None), P("ctx", "head", None), P("ctx", "head", None))
    return jax.shard_map(
        on_device, mesh=mesh, in_specs=in_specs, out_specs=out_specs, check_vma=False
    )
```

profile of v0, /device:TPU:0, one launch (start us, length us, event | category | flops | bytes accessed | tf_op | source)
XLA Modules:
  0.0 586.4 jit_solution(16674847419327355169)
XLA Ops:
  7.9 1.7 copy.164
  11.2 23.1 %all-gather = bf16[16,1,256]{2,1,0:T(2,128)(2,1)S(1)} all-gather(bf16[1,1,256]{2,1,0:T(2,128)(2,1)S(1)} %reshape.254), channel_id=1, replica_groups=mesh['ctx'=16,'head'=2] {'ctx'}, dimensions={0}, use_global_device_ids=true | all-gather | bytes 8704 | tf_op jit(solution)/shard_map/all_gather | solution.py:54
  40.2 1.8 compare_or_fusion.1
  41.9 1.8 compare_or_fusion
  43.7 1.7 all-gather.9.cloned.1.call-done
  45.4 10.9 %convolution_convert_fusion = bf16[256,2048]{1,0:T(8,128)(2,1)S(1)} fusion(bf16[256,4096]{1,0:T(8,128)(2,1)} %all-gather.9.cloned.1.call-done, bf16[2048,4096]{1,0:T(8,128)(2,1)} %param.11), kind=kOutput, calls=%fused_computation.55 | convolution fusion | flops 4295491584 | bytes 19922944 | tf_op jit(solution)/shard_map/dot_general | solution.py:42
  58.5 40.3 %all-gather.7.cloned.1.call-done = bf16[4096,4,128]{2,0,1:T(8,128)(2,1)} async-done(((bf16[256,4,128]{2,0,1:T(8,128)(2,1)}), bf16[4096,4,128]{2,0,1:T(8,128)(2,1)}) %all-gather.7.cloned.1.call-update) | async-done | bytes 4194320 | tf_op jit(solution)/shard_map/all_gather | solution.py:53
  98.8 4.7 copy.165
  103.5 3.2 gather_fusion.5
  106.7 4.9 gather_fusion.2
  111.6 38.4 %all-gather.5.cloned.1.call-done = bf16[4096,4,128]{2,1,0:T(4,128)(2,1)} async-done(((bf16[256,4,128]{2,1,0:T(4,128)(2,1)}), bf16[4096,4,128]{2,1,0:T(4,128)(2,1)}) %all-gather.5.cloned.1.call-update) | async-done | bytes 4194320 | tf_op jit(solution)/shard_map/all_gather | solution.py:52
  150.0 7.4 %gather_fusion = bf16[20,128,4,128]{3,2,1,0:T(4,128)(2,1)} fusion(bf16[32,128,4,128]{3,2,1,0:T(4,128)(2,1)} %bitcast.211, s32[1024]{0:T(1024)S(1)} %get-tuple-element.35), kind=kCustom, calls=%fused_computation | custom fusion | bytes 5242960 | tf_op jit(solution)/shard_map/gather | solution.py:66
  157.4 7.6 %gather_fusion.3 = bf16[20,128,4,128]{3,2,1,0:T(4,128)(2,1)} fusion(bf16[32,128,4,128]{3,2,1,0:T(4,128)(2,1)} %bitcast.212, s32[1024]{0:T(1024)S(1)} %get-tuple-element.34), kind=kCustom, calls=%fused_computation.3 | custom fusion | bytes 5242960 | tf_op jit(solution)/shard_map/gather | solution.py:66
  165.1 3.7 copy.166
  168.8 1.7 copy.175
  171.2 2.2 copy.162
  173.4 4.5 fusion.12
  177.9 4.3 fusion.15
  182.2 2.8 copy-done
  185.0 11.8 %fusion.38 = f32[2560,4,128]{0,2,1:T(8,128)} fusion(bf16[128,4,4,128]{0,3,2,1:T(8,128)(2,1)S(1)} %bitcast.226, f32[4,2560,128,4]{2,1,3,0:T(8,128)} %copy-done, f32[4,4,128]{2,1,0:T(4,128)S(1)} %bitcast.233, pred[128,2560]{0,1:T(8,128)(4,1)S(1)} %compare_or_fusion.1), kind=kOutput, calls=%fused_computation.53 | convolution fusion | flops 1363148800 | bytes 27074560 | tf_op jit(solution)/shard_map/gnij,ignd->jgd/dot_general | solution.py:26
  196.8 16.6 %fusion.61 = f32[128,4,4]{0,2,1:T(4,128)S(1)} fusion(bf16[2560,4,128,1]{2,0,3,1:T(8,128)(2,1)S(1)} %bitcast.221, f32[4,2560,128,4]{2,1,3,0:T(8,128)} %copy-done, f32[4,4,128]{2,1,0:T(4,128)S(1)} %bitcast.234, pred[128,2560]{0,1:T(8,128)(4,1)S(1)} %compare_or_fusion.1, bf16[128,4,4,128]{0,3,2,1:T(8,128)(2,1)S(1)} %bitcast.227), kind=kOutput, calls=%fused_computation.67 | convolution fusion | flops 8069576704 | bytes 24461312 | tf_op jit(solution)/shard_map/gnij,jgd->ignd/dot_general | solution.py:75
  213.5 15.1 %fusion.11 = bf16[4,4,128,2560]{2,3,1,0:T(8,128)(2,1)} fusion(f32[4,2560,128,4]{2,1,3,0:T(8,128)} %copy-done, f32[4,4,128]{2,1,0:T(4,128)S(1)} %bitcast.239, f32[4,4,128]{2,1,0:T(4,128)S(1)} %bitcast.235, pred[128,2560]{0,1:T(8,128)(4,1)S(1)} %compare_or_fusion.1, bf16[2560,4,128,1]{2,0,3,1:T(8,128)(2,1)S(1)} %bitcast.222, ...), kind=kOutput, calls=%fused_computation.26 | convolution fusion | flops 1378877440 | bytes 34947072 | tf_op jit(solution)/shard_map/ignd,jgd->gnij/dot_general | solution.py:27
  228.5 5.6 fusion.79
  234.1 2.9 copy.182
  237.1 6.3 %copy.186 = f32[2560,4,128]{2,0,1:T(8,128)} copy(f32[2560,4,128]{0,2,1:T(8,128)} %fusion.38) | data formatting | bytes 10485760 | tf_op jit(solution)/shard_map/gnij,ignd->jgd/transpose | solution.py:26
  243.4 5.5 copy.187
  248.9 3.0 fusion.3
  251.9 4.3 fusion.6
  256.2 2.8 copy-done.1
  259.0 11.9 %fusion.41 = f32[2560,4,128]{0,2,1:T(8,128)} fusion(bf16[128,4,4,128]{0,3,2,1:T(8,128)(2,1)S(1)} %bitcast.223, f32[4,2560,128,4]{2,1,3,0:T(8,128)} %copy-done.1, f32[4,4,128]{2,1,0:T(4,128)S(1)} %bitcast.236, pred[128,2560]{0,1:T(8,128)(4,1)S(1)} %compare_or_fusion), kind=kOutput, calls=%fused_computation.54 | convolution fusion | flops 1363148800 | bytes 27074560 | tf_op jit(solution)/shard_map/gnij,ignd->jgd/dot_general | solution.py:26
  270.8 16.8 %fusion.58 = f32[128,4,4]{0,2,1:T(4,128)S(1)} fusion(bf16[2560,4,128,1]{2,0,3,1:T(8,128)(2,1)S(1)} %bitcast.219, f32[4,2560,128,4]{2,1,3,0:T(8,128)} %copy-done.1, f32[4,4,128]{2,1,0:T(4,128)S(1)} %bitcast.237, pred[128,2560]{0,1:T(8,128)(4,1)S(1)} %compare_or_fusion, bf16[128,4,4,128]{0,3,2,1:T(8,128)(2,1)S(1)} %bitcast.224), kind=kOutput, calls=%fused_computation.66 | convolution fusion | flops 8069576704 | bytes 24461312 | tf_op jit(solution)/shard_map/gnij,jgd->ignd/dot_general | solution.py:75
  287.6 15.1 %fusion.2 = bf16[4,4,128,2560]{2,3,1,0:T(8,128)(2,1)} fusion(f32[4,2560,128,4]{2,1,3,0:T(8,128)} %copy-done.1, f32[4,4,128]{2,1,0:T(4,128)S(1)} %bitcast.240, f32[4,4,128]{2,1,0:T(4,128)S(1)} %bitcast.238, pred[128,2560]{0,1:T(8,128)(4,1)S(1)} %compare_or_fusion, bf16[2560,4,128,1]{2,0,3,1:T(8,128)(2,1)S(1)} %bitcast.220, ...), kind=kOutput, calls=%fused_computation.13 | convolution fusion | flops 1378877440 | bytes 34947072 | tf_op jit(solution)/shard_map/ignd,jgd->gnij/dot_general | solution.py:27
  302.7 5.6 fusion.80
  308.4 2.9 copy.183
  311.2 5.9 %copy.190 = f32[2560,4,128]{2,0,1:T(8,128)} copy(f32[2560,4,128]{0,2,1:T(8,128)} %fusion.41) | data formatting | bytes 10485760 | tf_op jit(solution)/shard_map/gnij,ignd->jgd/transpose | solution.py:26
  317.1 5.5 copy.191
  322.6 4.3 broadcast.69.clone.1
  326.9 13.9 %scatter_fusion = f32[32,128,4,128]{3,1,2,0:T(8,128)} fusion(f32[32,128,4,128]{3,1,2,0:T(8,128)} %broadcast.69.clone.1, s32[20]{0:T(128)S(1)} %copy-done.13, f32[20,128,4,128]{3,1,2,0:T(8,128)} %copy.182), kind=kCustom, calls=%fused_computation.6 | custom fusion | flops 1310720 | bytes 15728720 | tf_op jit(solution)/shard_map/scatter-add | solution.py:92
  340.8 4.4 broadcast.69.clone
  345.2 13.6 %scatter_fusion.2 = f32[32,128,4,128]{3,1,2,0:T(8,128)} fusion(f32[32,128,4,128]{3,1,2,0:T(8,128)} %broadcast.69.clone, s32[20]{0:T(128)S(1)} %copy-done.13, f32[20,128,4,128]{3,1,2,0:T(8,128)} %copy.187), kind=kCustom, calls=%fused_computation.8 | custom fusion | flops 1310720 | bytes 15728720 | tf_op jit(solution)/shard_map/scatter-add | solution.py:93
  358.8 13.6 %scatter_fusion.1 = f32[32,128,4,128]{3,1,2,0:T(8,128)} fusion(f32[32,128,4,128]{3,1,2,0:T(8,128)} %scatter_fusion, s32[20]{0:T(128)S(1)} %copy-done.11, f32[20,128,4,128]{3,1,2,0:T(8,128)} %copy.183), kind=kCustom, calls=%fused_computation.7 | custom fusion | flops 1310720 | bytes 15728720 | tf_op jit(solution)/shard_map/scatter-add | solution.py:92
  372.3 13.6 %scatter_fusion.3 = f32[32,128,4,128]{3,1,2,0:T(8,128)} fusion(f32[32,128,4,128]{3,1,2,0:T(8,128)} %scatter_fusion.2, s32[20]{0:T(128)S(1)} %copy-done.11, f32[20,128,4,128]{3,1,2,0:T(8,128)} %copy.191), kind=kCustom, calls=%fused_computation.9 | custom fusion | flops 1310720 | bytes 15728720 | tf_op jit(solution)/shard_map/scatter-add | solution.py:93
  386.0 6.6 %pad_maximum_fusion = f32[32,128,4,256]{3,1,2,0:T(8,128)S(1)} fusion(f32[32,128,4,128]{3,1,2,0:T(8,128)} %scatter_fusion.3, f32[32,128,4,128]{3,1,2,0:T(8,128)} %scatter_fusion.1), kind=kLoop, calls=%fused_computation.36 | loop fusion | flops 4194304 | bytes 33554432 | tf_op jit(solution)/shard_map/concatenate | solution.py:94
  392.6 6.1 %copy.192 = f32[32,128,4,256]{3,1,0,2:T(8,128)} copy(f32[32,128,4,256]{3,1,2,0:T(8,128)S(1)} %pad_maximum_fusion) | data formatting | bytes 33554432 | tf_op jit(solution)/shard_map/concatenate | solution.py:94
  398.7 8.7 %fusion.56 = bf16[1,128,4,4,128]{4,1,3,2,0:T(8,128)(2,1)S(1)} fusion(bf16[2560,4,128,1]{2,0,3,1:T(8,128)(2,1)} %bitcast.206, bf16[4,4,128,2560]{2,3,1,0:T(8,128)(2,1)} %fusion.11), kind=kOutput, calls=%fused_computation.64 | convolution fusion | flops 1342439424 | bytes 13631488 | tf_op jit(solution)/shard_map/gnij,jgd->ignd/dot_general | solution.py:29
  407.4 9.4 %fusion.57 = bf16[1,128,4,4,128]{4,1,3,2,0:T(8,128)(2,1)S(1)} fusion(bf16[2560,4,128,1]{2,0,3,1:T(8,128)(2,1)S(1)} %bitcast.204, bf16[4,4,128,2560]{2,3,1,0:T(8,128)(2,1)} %fusion.2), kind=kOutput, calls=%fused_computation.65 | convolution fusion | flops 1342439424 | bytes 13631488 | tf_op jit(solution)/shard_map/gnij,jgd->ignd/dot_general | solution.py:29
  417.0 1.7 copy.193
  418.7 157.6 %reduce-scatter.2.cloned.1.call-done = f32[256,4,256]{2,0,1:T(8,128)} async-done(((f32[4096,4,256]{2,0,1:T(8,128)}), f32[256,4,256]{2,0,1:T(8,128)}) %reduce-scatter.2.cloned.1.call-update) | async-done | bytes 1048592 | tf_op jit(solution)/shard_map/reduce_scatter | solution.py:97
  (62 shorter events, 14.4 us)
Async XLA Ops:
  7.2 38.2 %all-gather.9.cloned.1.call-start = ((), (), s32[]{:S(2)}) async-start(), calls=%async_computation.3 | async-start | bytes 3145728 | tf_op jit(solution)/shard_map/all_gather | solution.py:43
  7.9 90.9 %all-gather.7.cloned.1.call-start = ((), (), s32[]{:S(2)}) async-start(), calls=%async_computation.2 | async-start | bytes 4456448 | tf_op jit(solution)/shard_map/all_gather | solution.py:53
  9.7 140.4 %all-gather.5.cloned.1.call-start = ((), (), s32[]{:S(2)}) async-start(), calls=%async_computation.1 | async-start | bytes 4456448 | tf_op jit(solution)/shard_map/all_gather | solution.py:52
  10.4 565.9 %reduce-scatter.2.cloned.1.call-start = ((), (), s32[]{:S(2)}) async-start(), calls=%async_computation.4 | async-start | bytes 17825792 | tf_op jit(solution)/shard_map/reduce_scatter | solution.py:97
  35.1 0.6 copy-start.10
  35.1 0.6 copy-start.12
  165.1 5.4 copy-start.3
  165.1 6.1 %copy-start.2 = (bf16[20,128,4,128]{3,2,1,0:T(4,128)(2,1)S(1)}, bf16[20,128,4,128]{3,2,1,0:T(4,128)(2,1)}, u32[]{:S(2)}) copy-start(bf16[20,128,4,128]{3,2,1,0:T(4,128)(2,1)} %gather_fusion) | copy-start | bytes 7864324
  165.1 8.3 %copy-start.5 = (bf16[128,16,128]{2,0,1:T(8,128)(2,1)S(1)}, bf16[128,16,128]{2,0,1:T(8,128)(2,1)}, u32[]{:S(2)}) copy-start(bf16[128,16,128]{2,0,1:T(8,128)(2,1)} %copy.163) | copy-start | bytes 1572868
  177.9 7.1 %copy-start = (f32[4,2560,128,4]{2,1,3,0:T(8,128)}, f32[4,2560,128,4]{2,1,3,0:T(8,128)S(1)}, u32[]{:S(2)}) copy-start(f32[4,2560,128,4]{2,1,3,0:T(8,128)S(1)} %get-tuple-element.33) | copy-start | bytes 62914564
  177.9 7.1 %copy-start.9 = (bf16[128,2048]{0,1:T(8,128)(2,1)S(1)}, bf16[128,2048]{0,1:T(8,128)(2,1)}, u32[]{:S(2)}) copy-start(bf16[128,2048]{0,1:T(8,128)(2,1)} %copy.216) | copy-start | bytes 1572868
  185.0 11.8 %copy-start.7 = (bf16[20,128,4,128]{3,1,0,2:T(8,128)(2,1)S(1)}, bf16[20,128,4,128]{3,1,0,2:T(8,128)(2,1)}, u32[]{:S(2)}) copy-start(bf16[20,128,4,128]{3,1,0,2:T(8,128)(2,1)} %copy.166) | copy-start | bytes 7864324
  237.1 11.8 %copy-start.4 = (bf16[128,16,128]{2,0,1:T(8,128)(2,1)S(1)}, bf16[128,16,128]{2,0,1:T(8,128)(2,1)}, u32[]{:S(2)}) copy-start(bf16[128,16,128]{2,0,1:T(8,128)(2,1)} %copy.173) | copy-start | bytes 1572868
  251.8 7.1 %copy-start.1 = (f32[4,2560,128,4]{2,1,3,0:T(8,128)}, f32[4,2560,128,4]{2,1,3,0:T(8,128)S(1)}, u32[]{:S(2)}) copy-start(f32[4,2560,128,4]{2,1,3,0:T(8,128)S(1)} %get-tuple-element.31) | copy-start | bytes 62914564
  251.9 7.1 %copy-start.8 = (bf16[128,2048]{0,1:T(8,128)(2,1)S(1)}, bf16[128,2048]{0,1:T(8,128)(2,1)}, u32[]{:S(2)}) copy-start(bf16[128,2048]{0,1:T(8,128)(2,1)} %copy.217) | copy-start | bytes 1572868
  259.0 11.9 %copy-start.6 = (bf16[20,128,4,128]{3,1,0,2:T(8,128)(2,1)S(1)}, bf16[20,128,4,128]{3,1,0,2:T(8,128)(2,1)}, u32[]{:S(2)}) copy-start(bf16[20,128,4,128]{3,1,0,2:T(8,128)(2,1)} %copy.175) | copy-start | bytes 7864324
  317.1 9.8 %copy-start.13 = (s32[20]{0:T(128)S(1)}, s32[20]{0:T(128)}, u32[]{:S(2)}) copy-start(s32[20]{0:T(128)} %copy-done.12) | copy-start | bytes 244
  340.8 18.0 %copy-start.11 = (s32[20]{0:T(128)S(1)}, s32[20]{0:T(128)}, u32[]{:S(2)}) copy-start(s32[20]{0:T(128)} %copy-done.10) | copy-start | bytes 244
Sparse Core Ops, SparseCore 0:
  9.5 35.8 all-gather.8
  48.2 50.5 all-gather.6
  100.9 49.0 all-gather.4
  398.8 177.4 reduce-scatter.1
where the time goes:
time: 596 us; the launch traced here: 586 us
  waiting for transfers between devices  239 us (40%)
  matrix products  135 us (23%)
  local copies, waits for them, and re-layouts  98 us (16%)
  other arithmetic  76.3 us (13%)
  blocking collectives  23.1 us (4%)
  between operations  14.5 us (2%)
    reduce_scatter x1, waiting for transfers between devices, on_device(): home = lax.psum_scatter(combined, 'ctx', scatter_dimension=0, tiled=True)  158 us
    all_gather x1, waiting for transfers between devices, on_device(): lax.all_gather(value, 'ctx', axis=0, tiled=True)  40.3 us
    all_gather x1, waiting for transfers between devices, on_device(): lax.all_gather(key, 'ctx', axis=0, tiled=True)  38.4 us
    dot_general x2, matrix products, on_device(): jnp.einsum('gnij,jgd->ignd', probs, v_near.astype(jnp.float32), precision...  33.4 us
    dot_general x2, matrix products, backward_pair(): jnp.einsum('ignd,jgd->gnij', do_block, v_block, preferred_element_type=jn...  30.2 us
    scatter-add x2, other arithmetic, on_device(): grad_k_all.at[listed].add(part_k.reshape(slots, BLK, kv_here, width))  27.4 us
    scatter-add x2, other arithmetic, on_device(): grad_v_all.at[listed].add(part_v.reshape(slots, BLK, kv_here, width))  27.2 us
    dot_general x2, matrix products, backward_pair(): jnp.einsum('gnij,ignd->jgd', rounded, do_block, preferred_element_type=jn...  23.7 us
  transfers between devices with their start and end apart: 4, of which 4 were waited for; matrix products, arithmetic and copies ran while one was open for 10% of the time, Pallas kernels for 0%

commit v1 on v0

v1 whole, which is shorter than its diff:
```python
import functools
import math

import jax
import jax.numpy as jnp
from jax import lax
from jax.experimental import pallas as pl
from jax.experimental.pallas import tpu as pltpu
from jax.sharding import PartitionSpec as P

BLK = 128
PAD = 16
F32 = jnp.float32
BF16 = jnp.bfloat16
NT = (((1,), (1,)), ((), ()))
TN = (((0,), (0,)), ((), ()))


def attend_kernel(
    devices, tokens, kv, group, slots, listed, q_ref, do_ref, kv_ref, own_ref, gq_ref, part_ref,
    acc, s_scr, dp_scr, scope_scr, qg, dg, gq_acc,
):
    blocks = tokens // BLK
    width = BLK
    wide = group * BLK
    cut = next(c for c in (4, 2, 1) if slots % c == 0)
    chunk = cut * BLK
    scale = 1.0 / math.sqrt(width)
    log2e = scale * math.log2(math.e)

    def fill(d, _):
        tile = kv_ref[pl.ds(pl.multiple_of(d * (tokens + PAD) + tokens, PAD), PAD), 0:tokens]
        for b in range(blocks):
            row = tile[0:1, b * BLK : (b + 1) * BLK].astype(F32)
            at = pl.multiple_of((d * blocks + b) * BLK, BLK)
            scope_scr[pl.ds(at, BLK), :] = jnp.broadcast_to(row, (BLK, BLK)).T
        return 0

    lax.fori_loop(0, devices, fill, 0)

    def rows_of(j):
        d = j // blocks
        return pl.ds(pl.multiple_of(d * (tokens + PAD) + (j - d * blocks) * BLK, PAD), BLK)

    def head_loop(g, _):
        k_cols = pl.ds(pl.multiple_of(g * width, width), width)
        v_cols = pl.ds(pl.multiple_of((kv + g) * width, width), width)
        acc[...] = jnp.zeros_like(acc)

        def row_loop(r, _):
            q_rows = pl.ds(pl.multiple_of(r * BLK, BLK), BLK)

            def head_cols(n):
                return pl.ds(pl.multiple_of((g * group + n) * width, width), width)

            for n in range(group):
                qg[n * BLK : (n + 1) * BLK, :] = q_ref[q_rows, head_cols(n)]
                dg[n * BLK : (n + 1) * BLK, :] = do_ref[q_rows, head_cols(n)]
            own = own_ref[pl.ds(r, 1), :]

            def listed_rows(c):
                return [listed[r, c * cut + u] for u in range(cut)]

            def near(c, cols):
                return jnp.concatenate([kv_ref[rows_of(j), cols] for j in listed_rows(c)], axis=0)

            def here(c):
                return pl.ds(pl.multiple_of(c * chunk, chunk), chunk)

            def first(c, high):
                s = lax.dot_general(near(c, k_cols), qg[...], NT, preferred_element_type=F32)
                bias = []
                for j in listed_rows(c):
                    sk = scope_scr[pl.ds(pl.multiple_of(j * BLK, BLK), BLK), :]
                    b = jnp.where((sk == own) | (sk == 0.0), 0.0, -1e30)
                    bias.append(jnp.concatenate([b] * group, axis=1))
                s = s + jnp.concatenate(bias, axis=0)
                s_scr[here(c), :] = s
                return jnp.maximum(high, jnp.max(s, axis=0, keepdims=True))

            high = lax.fori_loop(0, slots // cut, first, jnp.full((1, wide), -1e30, F32))

            def second(c, carry):
                total, delta = carry
                p = jnp.exp2((s_scr[here(c), :] - high) * log2e)
                dp = lax.dot_general(near(c, v_cols), dg[...], NT, preferred_element_type=F32)
                s_scr[here(c), :] = p
                dp_scr[here(c), :] = dp
                return (
                    total + jnp.sum(p, axis=0, keepdims=True),
                    delta + jnp.sum(p * dp, axis=0, keepdims=True),
                )

            zero = jnp.zeros((1, wide), F32)
            total, delta = lax.fori_loop(0, slots // cut, second, (zero, zero))
            inverse = 1.0 / total
            delta = delta * inverse
            gq_acc[...] = jnp.zeros_like(gq_acc)

            def third(c, _):
                pn = s_scr[here(c), :] * inverse
                ds = (pn * ((dp_scr[here(c), :] - delta) * scale)).astype(BF16)
                gv = jnp.dot(pn.astype(BF16), dg[...], preferred_element_type=F32)
                gk = jnp.dot(ds, qg[...], preferred_element_type=F32)
                gq_acc[...] += lax.dot_general(near(c, k_cols), ds, TN, preferred_element_type=F32)
                for u, j in enumerate(listed_rows(c)):
                    at = pl.ds(pl.multiple_of(j * BLK, BLK), BLK)
                    acc[at, 0:width] += gk[u * BLK : (u + 1) * BLK, :]
                    acc[at, width : 2 * width] += gv[u * BLK : (u + 1) * BLK, :]
                return 0

            lax.fori_loop(0, slots // cut, third, 0)
            for n in range(group):
                gq_ref[q_rows, head_cols(n)] = gq_acc[:, n * BLK : (n + 1) * BLK].T.astype(BF16)
            return 0

        lax.fori_loop(0, blocks, row_loop, 0)
        part_ref[:, k_cols] = acc[:, 0:width].astype(BF16)
        part_ref[:, v_cols] = acc[:, width : 2 * width].astype(BF16)
        return 0

    lax.fori_loop(0, kv, head_loop, 0)


def attend(listed, q, do, kv_all, own, devices, kv):
    tokens = q.shape[0]
    group = q.shape[1] // BLK // kv
    slots = listed.shape[1]
    total = devices * tokens
    wide = group * BLK
    vmem = pl.BlockSpec(memory_space=pltpu.VMEM)
    return pl.pallas_call(
        functools.partial(attend_kernel, devices, tokens, kv, group, slots),
        out_shape=(
            jax.ShapeDtypeStruct(q.shape, BF16),
            jax.ShapeDtypeStruct((total, 2 * kv * BLK), BF16),
        ),
        in_specs=[pl.BlockSpec(memory_space=pltpu.SMEM)] + [vmem] * 4,
        out_specs=(vmem, vmem),
        scratch_shapes=[
            pltpu.VMEM((total, 2 * BLK), F32),
            pltpu.VMEM((slots * BLK, wide), F32),
            pltpu.VMEM((slots * BLK, wide), F32),
            pltpu.VMEM((total, BLK), F32),
            pltpu.VMEM((wide, BLK), BF16),
            pltpu.VMEM((wide, BLK), BF16),
            pltpu.VMEM((BLK, wide), F32),
        ],
        compiler_params=pltpu.CompilerParams(vmem_limit_bytes=56 * 2**20),
        name="attend",
    )(listed, q, do, kv_all, own)


def on_device(devices, query, key, value, d_mixed, out_weight, block_keys, scope_ids):
    tokens, heads, width = query.shape
    kv = key.shape[1]
    cols = 2 * kv * width
    scope_rows = jnp.zeros((PAD, cols), BF16).at[:, :tokens].set(scope_ids.astype(BF16)[None, :])
    block = jnp.concatenate(
        [
            jnp.concatenate([key.reshape(tokens, -1), value.reshape(tokens, -1)], axis=1),
            scope_rows,
        ],
        axis=0,
    )
    kv_all = lax.all_gather(block, "ctx", axis=0, tiled=True)
    d_out = lax.dot_general(
        lax.all_gather(d_mixed, "head", axis=1, tiled=True),
        out_weight,
        NT,
        preferred_element_type=F32,
    ).astype(BF16)
    own = scope_ids.astype(F32).reshape(tokens // BLK, BLK)
    grad_q, part = attend(
        block_keys, query.reshape(tokens, -1), d_out, kv_all, own, devices, kv
    )
    home = lax.psum_scatter(part, "ctx", scatter_dimension=0, tiled=True)
    half = kv * width
    return (
        grad_q.reshape(query.shape),
        home[:, :half].reshape(key.shape),
        home[:, half:].reshape(value.shape),
    )


def solution(mesh):
    in_specs = (
        P("ctx", "head", None),
        P("ctx", "head", None),
        P("ctx", "head", None),
        P("ctx", "head"),
        P("head", None),
        P("ctx", None),
        P("ctx"),
    )
    out_specs = (P("ctx", "head", None), P("ctx", "head", None), P("ctx", "head", None))
    return jax.shard_map(
        functools.partial(on_device, mesh.shape["ctx"]),
        mesh=mesh,
        in_specs=in_specs,
        out_specs=out_specs,
        check_vma=False,
    )
```

time: 596 us -> 299 us (0.50); the launches traced: 586 us -> 299 us
  matrix products: 135 us -> 11.9 us
  local copies, waits for them, and re-layouts: 98 us -> 7.36 us
  other arithmetic: 76.3 us -> 3.41 us
  Pallas kernels: 0 us -> 61.2 us
  waiting for transfers between devices: 239 us -> 201 us
  blocking collectives: 23.1 us -> 0 us
    dot_general x12 -> x0, matrix products: 124 us -> none  [the longest x2 33.4 us: on_device(): jnp.einsum('gnij,jgd->ignd', probs, v_near.astype(jnp.float32), precision...]
    pallas_call x0 -> x1, Pallas kernels: none -> 61.2 us  [attend(): pl.pallas_call(functools.partial(attend_kernel, devices, tokens, kv, grou...]
    reduce_scatter x1, waiting for transfers between devices: 158 us -> 101 us  [on_device(): home = lax.psum_scatter(part, 'ctx', scatter_dimension=0, tiled=True)]
    scatter-add x4 -> x0, other arithmetic: 54.7 us -> none  [the longest x2 27.4 us: on_device(): grad_k_all.at[listed].add(part_k.reshape(slots, BLK, kv_here, width))]
    gather x10 -> x0, local copies, waits for them, and re-layouts: 32.6 us -> none  [the longest x4 17.9 us: on_device(): k_near = k_all[listed].reshape(slots * BLK, kv_here, width)]
    all_gather x1, waiting for transfers between devices: 1.71 us -> 31.6 us  [on_device(): lax.all_gather(d_mixed, 'head', axis=1, tiled=True)]
    all_gather x1 -> x0, blocking collectives: 23.1 us -> none  [on_device(): lax.all_gather(scope_ids.astype(jnp.bfloat16), 'ctx', axis=0, tiled=True)]
    reshape x6 -> x3, local copies, waits for them, and re-layouts: 21.5 us -> 2.62 us  [the longest x1 1.09 us: on_device(): value.reshape(tokens, -1)]
  transfers between devices with their start and end apart: 4 -> 3, of which waited for: 4 -> 3; matrix products, arithmetic and copies ran while one was open for 10% -> 6% of each run, Pallas kernels for 0% -> 0%
where the time goes in v1:
time: 299 us
  waiting for transfers between devices  201 us (67%)
  Pallas kernels  61.2 us (20%)
  between operations  13.8 us (5%)
  matrix products  11.9 us (4%)
  local copies, waits for them, and re-layouts  7.36 us (2%)
  other arithmetic  3.41 us (1%)
    reduce_scatter x1, waiting for transfers between devices, on_device(): home = lax.psum_scatter(part, 'ctx', scatter_dimension=0, tiled=True)  101 us
    all_gather x1, waiting for transfers between devices, on_device(): kv_all = lax.all_gather(block, 'ctx', axis=0, tiled=True)  68.6 us
    pallas_call x1, Pallas kernels, attend(): pl.pallas_call(functools.partial(attend_kernel, devices, tokens, kv, grou...  61.2 us
    all_gather x1, waiting for transfers between devices, on_device(): lax.all_gather(d_mixed, 'head', axis=1, tiled=True)  31.6 us
    dot_general x1, matrix products, on_device(): lax.dot_general(lax.all_gather(d_mixed, 'head', axis=1, tiled=True), out_...  11.9 us
  transfers between devices with their start and end apart: 3, of which 3 were waited for; matrix products, arithmetic and copies ran while one was open for 6% of the time, Pallas kernels for 0%

profile of v1, /device:TPU:0, one launch (start us, length us, event | category | flops | bytes accessed | tf_op | source)
XLA Modules:
  0.0 299.1 jit_solution(13692137056180806986)
XLA Ops:
  7.2 0.0 copy-start
  7.2 0.0 all-gather.3.cloned.1.call-start
  7.2 0.7 all-gather.3.cloned.1.call-update
  7.9 0.0 all-gather.5.cloned.1.call-start
  8.0 0.6 compare_reduce_fusion
  8.6 1.3 broadcast_select_fusion
  9.9 1.1 copy_bitcast_fusion.1
  11.0 0.0 copy-start.2
  11.1 0.9 pad_maximum_fusion
  11.9 0.0 all-gather.5.cloned.1.call-update
  12.0 0.0 reduce-scatter.2.cloned.1.call-start
  12.0 0.0 copy-done
  12.0 1.2 copy.17
  13.3 0.0 copy-done.2
  13.3 0.6 convert_bitcast_fusion.own_ref
  13.8 31.6 %all-gather.3.cloned.1.call-done = bf16[256,4096]{1,0:T(8,128)(2,1)} async-done(((bf16[256,2048]{1,0:T(8,128)(2,1)}), bf16[256,4096]{1,0:T(8,128)(2,1)}) %all-gather.3.cloned.1.call-update) | async-done | bytes 2097168 | tf_op jit(solution)/shard_map/all_gather | solution.py:168
  45.4 11.9 %convolution_convert_fusion.do_ref = bf16[256,2048]{1,0:T(8,128)(2,1)} fusion(bf16[256,4096]{1,0:T(8,128)(2,1)} %all-gather.3.cloned.1.call-done, bf16[2048,4096]{1,0:T(8,128)(2,1)} %param.13), kind=kOutput, calls=%fused_computation | convolution fusion | flops 4295491584 | bytes 19922944 | tf_op jit(solution)/shard_map/dot_general | solution.py:167
  57.3 68.6 %all-gather.5.cloned.1.call-done.kv_ref = bf16[4352,1024]{1,0:T(8,128)(2,1)} async-done(((bf16[272,1024]{1,0:T(8,128)(2,1)}), bf16[4352,1024]{1,0:T(8,128)(2,1)}) %all-gather.5.cloned.1.call-update) | async-done | bytes 8912912 | tf_op jit(solution)/shard_map/all_gather | solution.py:166
  125.9 61.2 %attend.1 = (bf16[256,2048]{1,0:T(8,128)(2,1)}, bf16[4096,1024]{1,0:T(8,128)(2,1)}) custom-call(s32[2,20]{1,0:T(2,128)} %listed.1, bf16[256,2048]{1,0:T(8,128)(2,1)} %bitcast.16, bf16[256,2048]{1,0:T(8,128)(2,1)} %convolution_convert_fusion.do_ref, bf16[4352,1024]{1,0:T(8,128)(2,1)} %all-gather.5.cloned.1.call-done.kv_ref, f32[2,128]{1,0:T(2,128)} %convert_bitcast_fusion.own_ref), custom_call_target="tpu_custom_call" | custom-call | tf_op jit(solution)/shard_map/attend/pallas_call | solution.py:132
  187.1 0.0 copy-start.1
  187.1 0.0 reduce-scatter.2.cloned.1.call-update
  187.1 1.2 copy-done.1
  188.3 1.2 copy.13
  189.5 100.5 %reduce-scatter.2.cloned.1.call-done = bf16[256,1024]{1,0:T(8,128)(2,1)} async-done(((bf16[4096,1024]{1,0:T(8,128)(2,1)}), bf16[256,1024]{1,0:T(8,128)(2,1)}) %reduce-scatter.2.cloned.1.call-update) | async-done | bytes 524304 | tf_op jit(solution)/shard_map/reduce_scatter | solution.py:177
  290.0 1.1 fusion
  291.1 0.8 reshape.58
  291.8 0.8 reshape.57
  (2 shorter events, 0.0 us)
Async XLA Ops:
  7.2 4.8 %copy-start = (bf16[256,16,128]{2,1,0:T(8,128)(2,1)S(1)}, bf16[256,16,128]{2,1,0:T(8,128)(2,1)}, u32[]{:S(2)}) copy-start(bf16[256,16,128]{2,1,0:T(8,128)(2,1)} %param.9) | copy-start | bytes 3145732
  7.2 38.2 %all-gather.3.cloned.1.call-start = ((), (), s32[]{:S(2)}) async-start(), calls=%async_computation.1 | async-start | bytes 3145728 | tf_op jit(solution)/shard_map/all_gather | solution.py:168
  7.9 118.0 %all-gather.5.cloned.1.call-start = ((), (), s32[]{:S(2)}) async-start(), calls=%async_computation.2 | async-start | bytes 9469952 | tf_op jit(solution)/shard_map/all_gather | solution.py:166
  11.0 2.2 copy-start.2
  12.0 278.1 %reduce-scatter.2.cloned.1.call-start = ((), (), s32[]{:S(2)}) async-start(), calls=%async_computation.3 | async-start | bytes 8912896 | tf_op jit(solution)/shard_map/reduce_scatter | solution.py:177
  187.1 1.2 copy-start.1
Sparse Core Ops, SparseCore 0:
  9.6 35.8 all-gather.2
  47.7 78.1 all-gather.4
  187.2 102.7 reduce-scatter.1

commit v2 on v1

--- a/solution.py
+++ b/solution.py
@@ -14,6 +14,7 @@
 BF16 = jnp.bfloat16
 NT = (((1,), (1,)), ((), ()))
 TN = (((0,), (0,)), ((), ()))
+MESH = pl.DeviceIdType.MESH
 
 
 def attend_kernel(
@@ -151,7 +152,225 @@
     )(listed, q, do, kv_all, own)
 
 
-def on_device(devices, query, key, value, d_mixed, out_weight, block_keys, scope_ids):
+def place(devices):
+    me = lax.axis_index("ctx")
+    a, b, c = me // 4, lax.rem(me // 2, 2), lax.rem(me, 2)
+    return a, b, c, devices // 4
+
+
+def greet(ctx_peers, head_peers):
+    barrier = pltpu.get_barrier_semaphore()
+    for peer in ctx_peers:
+        pl.semaphore_signal(barrier, inc=1, device_id={"ctx": peer}, device_id_type=MESH)
+    for peer in head_peers:
+        pl.semaphore_signal(barrier, inc=1, device_id={"head": peer}, device_id_type=MESH)
+    pl.semaphore_wait(barrier, len(ctx_peers) + len(head_peers))
+
+
+def near_first(count):
+    return sorted(range(1, count), key=lambda o: min(o, count - o))
+
+
+def gather_kernel(
+    devices, heads, block_ref, mixed_ref, all_ref, wide_ref,
+    z_send, z_recv, x_send, x_recv, c_send, c_recv, h_send, h_recv, own_sem,
+):
+    rows = block_ref.shape[0]
+    width = mixed_ref.shape[1]
+    a, b, c, count = place(devices)
+    head = lax.axis_index("head")
+    order = near_first(count)
+
+    def index(o, far, other):
+        far_a = lax.rem(a - o + count, count)
+        return far_a * 4 + ((1 - b) if far else b) * 2 + ((1 - c) if other else c)
+
+    def slot(i):
+        return all_ref.at[pl.ds(pl.multiple_of(i * rows, PAD), rows)]
+
+    def cols(h):
+        return wide_ref.at[:, pl.ds(pl.multiple_of(h * width, BLK), width)]
+
+    z_peers = {o: lax.rem(a + o, count) * 4 + b * 2 + c for o in order}
+    x_peer = a * 4 + (1 - b) * 2 + c
+    c_peer = a * 4 + b * 2 + (1 - c)
+    h_peers = {o: lax.rem(head + o, heads) for o in range(1, heads)}
+    greet([z_peers[o] for o in order] + [x_peer, c_peer], list(h_peers.values()))
+
+    def copy(src, dst, send, recv, where):
+        return pltpu.make_async_remote_copy(
+            src_ref=src, dst_ref=dst, send_sem=send, recv_sem=recv,
+            device_id=where, device_id_type=MESH,
+        )
+
+    sent = []
+
+    def send(*args):
+        out = copy(*args)
+        out.start()
+        sent.append(out)
+
+    mine = slot(index(0, False, False))
+    keep = pltpu.make_async_copy(block_ref, mine, own_sem.at[0])
+    keep.start()
+    keep_mixed = pltpu.make_async_copy(mixed_ref, cols(head), own_sem.at[1])
+    keep_mixed.start()
+    send(block_ref, mine, x_send.at[0], x_recv.at[0], {"ctx": x_peer})
+    for o in order:
+        send(block_ref, mine, z_send.at[o], z_recv.at[o], {"ctx": z_peers[o]})
+    for o in range(1, heads):
+        send(mixed_ref, cols(head), h_send.at[o], h_recv.at[o], {"head": h_peers[o]})
+    send(block_ref, mine, c_send.at[0], c_recv.at[0], {"ctx": c_peer})
+
+    def arrived(ref, sem, where):
+        copy(ref, ref, own_sem.at[2], sem, where).wait_recv()
+
+    def over_x(o):
+        got = slot(index(o, True, False))
+        arrived(got, x_recv.at[o], {"ctx": x_peer})
+        at = 2 * o + 1
+        send(got, got, c_send.at[at], c_recv.at[at], {"ctx": c_peer})
+
+    before = 0
+    for o in order:
+        got = slot(index(o, False, False))
+        arrived(got, z_recv.at[o], {"ctx": z_peers[o]})
+        send(got, got, x_send.at[o], x_recv.at[o], {"ctx": x_peer})
+        send(got, got, c_send.at[2 * o], c_recv.at[2 * o], {"ctx": c_peer})
+        over_x(before)
+        before = o
+    over_x(before)
+    for o in range(count):
+        for far in (False, True):
+            at = 2 * o + int(far)
+            arrived(slot(index(o, far, True)), c_recv.at[at], {"ctx": c_peer})
+    for o in range(1, heads):
+        arrived(cols(lax.rem(head - o + heads, heads)), h_recv.at[o], {"head": h_peers[o]})
+    for out in sent:
+        out.wait_send()
+    keep.wait()
+    keep_mixed.wait()
+
+
+def gather(block, d_mixed, devices, heads):
+    count = devices // 4
+    dma = pltpu.SemaphoreType.DMA
+    hbm = pl.BlockSpec(memory_space=pl.ANY)
+    return pl.pallas_call(
+        functools.partial(gather_kernel, devices, heads),
+        out_shape=(
+            jax.ShapeDtypeStruct((devices * block.shape[0], block.shape[1]), BF16),
+            jax.ShapeDtypeStruct((d_mixed.shape[0], heads * d_mixed.shape[1]), BF16),
+        ),
+        in_specs=[hbm, hbm],
+        out_specs=(hbm, hbm),
+        scratch_shapes=[
+            dma((count,)), dma((count,)), dma((count,)), dma((count,)),
+            dma((2 * count,)), dma((2 * count,)), dma((heads,)), dma((heads,)), dma((3,)),
+        ],
+        compiler_params=pltpu.CompilerParams(collective_id=0, has_side_effects=True),
+        name="gather",
+    )(block, d_mixed)
+
+
+def scatter_kernel(
+    devices, part_ref, home_ref, c_land, x_land, z_land, x_out, z_out,
+    c_send, c_recv, x_send, x_recv, z_send, z_recv,
+):
+    rows = home_ref.shape[0]
+    step = 32
+    a, b, c, count = place(devices)
+    order = near_first(count)[::-1] + [0]
+
+    def part_at(o, far, other):
+        i = lax.rem(a + o, count) * 4 + ((1 - b) if far else b) * 2 + ((1 - c) if other else c)
+        return pl.multiple_of(i * rows, rows)
+
+    z_peers = {o: lax.rem(a + o, count) * 4 + b * 2 + c for o in range(1, count)}
+    x_peer = a * 4 + (1 - b) * 2 + c
+    c_peer = a * 4 + b * 2 + (1 - c)
+    greet(list(z_peers.values()) + [x_peer, c_peer], [])
+
+    def copy(src, dst, send, recv, peer):
+        return pltpu.make_async_remote_copy(
+            src_ref=src, dst_ref=dst, send_sem=send, recv_sem=recv,
+            device_id={"ctx": peer}, device_id_type=MESH,
+        )
+
+    core, across, along = {}, {}, {}
+    for far in (True, False):
+        for o in order:
+            at = 2 * o + int(far)
+            core[at] = copy(
+                part_ref.at[pl.ds(part_at(o, far, True), rows)], c_land.at[at],
+                c_send.at[at], c_recv.at[at], c_peer,
+            )
+            core[at].start()
+
+    def add(out, at, terms):
+        def body(i, _):
+            here = pl.multiple_of(i * step, step)
+            total = part_ref[pl.ds(at + here, step), :].astype(F32)
+            for land, index in terms:
+                total = total + land[index, pl.ds(here, step), :].astype(F32)
+            out[pl.ds(here, step), :] = total.astype(BF16)
+            return 0
+
+        lax.fori_loop(0, rows // step, body, 0)
+
+    for o in order:
+        at = 2 * o + 1
+        core[at].wait_recv()
+        add(x_out.at[o], part_at(o, True, False), [(c_land, at)])
+        across[o] = copy(x_out.at[o], x_land.at[o], x_send.at[o], x_recv.at[o], x_peer)
+        across[o].start()
+    for o in order:
+        core[2 * o].wait_recv()
+        across[o].wait_recv()
+        terms = [(c_land, 2 * o), (x_land, o)]
+        if o > 0:
+            add(z_out.at[o], part_at(o, False, False), terms)
+            along[o] = copy(z_out.at[o], z_land.at[o], z_send.at[o], z_recv.at[o], z_peers[o])
+            along[o].start()
+    for o in order[:-1]:
+        along[o].wait_recv()
+    add(
+        home_ref,
+        part_at(0, False, False),
+        [(c_land, 0), (x_land, 0)] + [(z_land, o) for o in range(1, count)],
+    )
+    for made in (core, across, along):
+        for out in made.values():
+            out.wait_send()
+
+
+def scatter(part, devices):
+    count = devices // 4
+    dma = pltpu.SemaphoreType.DMA
+    vmem = pl.BlockSpec(memory_space=pltpu.VMEM)
+    block = (part.shape[0] // devices, part.shape[1])
+    return pl.pallas_call(
+        functools.partial(scatter_kernel, devices),
+        out_shape=jax.ShapeDtypeStruct(block, BF16),
+        in_specs=[vmem],
+        out_specs=vmem,
+        scratch_shapes=[
+            pltpu.VMEM((2 * count,) + block, BF16),
+            pltpu.VMEM((count,) + block, BF16),
+            pltpu.VMEM((count,) + block, BF16),
+            pltpu.VMEM((count,) + block, BF16),
+            pltpu.VMEM((count,) + block, BF16),
+            dma((2 * count,)), dma((2 * count,)),
+            dma((count,)), dma((count,)), dma((count,)), dma((count,)),
+        ],
+        compiler_params=pltpu.CompilerParams(
+            collective_id=1, has_side_effects=True, vmem_limit_bytes=40 * 2**20
+        ),
+        name="scatter",
+    )(part)
+
+
+def on_device(devices, split, query, key, value, d_mixed, out_weight, block_keys, scope_ids):
     tokens, heads, width = query.shape
     kv = key.shape[1]
     cols = 2 * kv * width
@@ -163,9 +382,9 @@
         ],
         axis=0,
     )
-    kv_all = lax.all_gather(block, "ctx", axis=0, tiled=True)
+    kv_all, mixed = gather(block, d_mixed, devices, split)
     d_out = lax.dot_general(
-        lax.all_gather(d_mixed, "head", axis=1, tiled=True),
+        mixed,
         out_weight,
         NT,
         preferred_element_type=F32,
@@ -174,7 +393,7 @@
     grad_q, part = attend(
         block_keys, query.reshape(tokens, -1), d_out, kv_all, own, devices, kv
     )
-    home = lax.psum_scatter(part, "ctx", scatter_dimension=0, tiled=True)
+    home = scatter(part, devices)
     half = kv * width
     return (
         grad_q.reshape(query.shape),
@@ -195,7 +414,7 @@
     )
     out_specs = (P("ctx", "head", None), P("ctx", "head", None), P("ctx", "head", None))
     return jax.shard_map(
-        functools.partial(on_device, mesh.shape["ctx"]),
+        functools.partial(on_device, mesh.shape["ctx"], mesh.shape["head"]),
         mesh=mesh,
         in_specs=in_specs,
         out_specs=out_specs,

time: 299 us -> 222 us (0.74)
  waiting for transfers between devices: 201 us -> 0 us
  Pallas kernels: 61.2 us -> 195 us
  between operations: 13.8 us -> 0.67 us
    pallas_call x0 -> x2, Pallas kernels: none -> 134 us  [the longest x1 70.1 us: gather(): pl.pallas_call(functools.partial(gather_kernel, devices, heads), out_shap...]
    reduce_scatter x1 -> x0, waiting for transfers between devices: 101 us -> none  [on_device(): home = lax.psum_scatter(part, 'ctx', scatter_dimension=0, tiled=True)]
    all_gather x2 -> x0, waiting for transfers between devices: 100 us -> none  [the longest x1 68.6 us: on_device(): kv_all = lax.all_gather(block, 'ctx', axis=0, tiled=True)]
    unnamed x8 -> x6, local copies, waits for them, and re-layouts: 3.66 us -> 7.06 us
  transfers between devices with their start and end apart: 3 -> 0, of which waited for: 3 -> 0; matrix products, arithmetic and copies ran while one was open for 6% -> 0% of each run, Pallas kernels for 0% -> 0%
where the time goes in v2:
time: 222 us
  Pallas kernels  195 us (88%)
  matrix products  11.9 us (5%)
  local copies, waits for them, and re-layouts  9.73 us (4%)
  other arithmetic  4.09 us (2%)
    pallas_call x1, Pallas kernels, gather(): pl.pallas_call(functools.partial(gather_kernel, devices, heads), out_shap...  70.1 us
    pallas_call x1, Pallas kernels, scatter(): pl.pallas_call(functools.partial(scatter_kernel, devices), out_shape=jax....  63.9 us
    pallas_call x1, Pallas kernels, attend(): pl.pallas_call(functools.partial(attend_kernel, devices, tokens, kv, grou...  61.2 us
    dot_general x1, matrix products, on_device(): lax.dot_general(mixed, out_weight, NT, preferred_element_type=F32)  11.9 us
    unnamed x6, local copies, waits for them, and re-layouts  7.06 us

profile of v2, /device:TPU:0, one launch (start us, length us, event | category | flops | bytes accessed | tf_op | source)
XLA Modules:
  0.0 221.5 jit_solution(2430687970195258891)
XLA Ops:
  0.6 0.0 copy-start.1
  0.6 0.6 compare_reduce_fusion
  1.3 1.3 broadcast_select_fusion
  2.6 1.2 convert_bitcast_fusion.own_ref
  3.9 1.1 copy_bitcast_fusion.1
  5.0 0.9 pad_maximum_fusion.block_ref
  5.8 0.0 copy-done.1
  5.8 1.2 copy.17
  7.1 70.1 %gather.1 = (bf16[4352,1024]{1,0:T(8,128)(2,1)}, bf16[256,4096]{1,0:T(8,128)(2,1)}) custom-call(bf16[272,1024]{1,0:T(8,128)(2,1)} %pad_maximum_fusion.block_ref, bf16[256,2048]{1,0:T(8,128)(2,1)} %mixed_ref.1), custom_call_target="tpu_custom_call" | custom-call | tf_op jit(solution)/shard_map/gather/pallas_call | solution.py:259
  77.2 11.9 %convolution_convert_fusion.do_ref = bf16[256,2048]{1,0:T(8,128)(2,1)} fusion(bf16[256,4096]{1,0:T(8,128)(2,1)} %get-tuple-element.19, bf16[2048,4096]{1,0:T(8,128)(2,1)} %param.13), kind=kOutput, calls=%fused_computation | convolution fusion | flops 4295491584 | bytes 19922944 | tf_op jit(solution)/shard_map/dot_general | solution.py:386
  89.1 61.2 %attend.1 = (bf16[256,2048]{1,0:T(8,128)(2,1)}, bf16[4096,1024]{1,0:T(8,128)(2,1)}) custom-call(s32[2,20]{1,0:T(2,128)} %listed.1, bf16[256,2048]{1,0:T(8,128)(2,1)} %bitcast.16, bf16[256,2048]{1,0:T(8,128)(2,1)} %convolution_convert_fusion.do_ref, bf16[4352,1024]{1,0:T(8,128)(2,1)} %get-tuple-element.20.kv_ref, f32[2,128]{1,0:T(2,128)} %convert_bitcast_fusion.own_ref), custom_call_target="tpu_custom_call" | custom-call | tf_op jit(solution)/shard_map/attend/pallas_call | solution.py:133
  150.3 2.4 %copy.13 = bf16[32,8,16,128]{3,2,1,0:T(8,128)(2,1)} copy(bf16[32,8,16,128]{3,1,2,0:T(8,128)(2,1)} %bitcast.19) | data formatting | bytes 2097152
  152.7 0.0 copy-start
  152.7 3.4 %copy-done = bf16[4096,1024]{1,0:T(8,128)(2,1)S(1)} copy-done((bf16[4096,1024]{1,0:T(8,128)(2,1)S(1)}, bf16[4096,1024]{1,0:T(8,128)(2,1)}, u32[]{:S(2)}) %copy-start) | copy-done | bytes 8388632
  156.1 63.9 %scatter.10 = bf16[256,1024]{1,0:T(8,128)(2,1)S(1)} custom-call(bf16[4096,1024]{1,0:T(8,128)(2,1)S(1)} %copy-done), custom_call_target="tpu_custom_call" | custom-call | tf_op jit(solution)/shard_map/scatter/pallas_call | solution.py:352
  220.0 0.8 reshape.58
  220.8 0.8 reshape.57
  (3 shorter events, 0.0 us)
Async XLA Ops:
  0.6 5.2 %copy-start.1 = (bf16[256,16,128]{2,1,0:T(8,128)(2,1)S(1)}, bf16[256,16,128]{2,1,0:T(8,128)(2,1)}, u32[]{:S(2)}) copy-start(bf16[256,16,128]{2,1,0:T(8,128)(2,1)} %param.9) | copy-start | bytes 3145732
  152.7 3.4 %copy-start = (bf16[4096,1024]{1,0:T(8,128)(2,1)S(1)}, bf16[4096,1024]{1,0:T(8,128)(2,1)}, u32[]{:S(2)}) copy-start(bf16[4096,1024]{1,0:T(8,128)(2,1)} %get-tuple-element.22.part_ref) | copy-start | bytes 25165828

commit v3 on v2

--- a/solution.py
+++ b/solution.py
@@ -172,30 +172,39 @@
 
 
 def gather_kernel(
-    devices, heads, block_ref, mixed_ref, all_ref, wide_ref,
+    devices, heads, block_ref, mixed_ref, weight_ref, all_ref, do_ref, wide, weight,
     z_send, z_recv, x_send, x_recv, c_send, c_recv, h_send, h_recv, own_sem,
 ):
     rows = block_ref.shape[0]
     width = mixed_ref.shape[1]
     a, b, c, count = place(devices)
     head = lax.axis_index("head")
-    order = near_first(count)
-
-    def index(o, far, other):
-        far_a = lax.rem(a - o + count, count)
-        return far_a * 4 + ((1 - b) if far else b) * 2 + ((1 - c) if other else c)
-
-    def slot(i):
-        return all_ref.at[pl.ds(pl.multiple_of(i * rows, PAD), rows)]
-
-    def cols(h):
-        return wide_ref.at[:, pl.ds(pl.multiple_of(h * width, BLK), width)]
-
-    z_peers = {o: lax.rem(a + o, count) * 4 + b * 2 + c for o in order}
     x_peer = a * 4 + (1 - b) * 2 + c
     c_peer = a * 4 + b * 2 + (1 - c)
     h_peers = {o: lax.rem(head + o, heads) for o in range(1, heads)}
-    greet([z_peers[o] for o in order] + [x_peer, c_peer], list(h_peers.values()))
+
+    def slot(at, far, other):
+        i = at * 4 + ((1 - b) if far else b) * 2 + ((1 - c) if other else c)
+        return all_ref.at[pl.ds(pl.multiple_of(i * rows, PAD), rows)]
+
+    def cols(h):
+        return wide.at[:, pl.ds(pl.multiple_of(h * width, BLK), width)]
+
+    barrier = pltpu.get_barrier_semaphore()
+    for way in (1, -1):
+
+        @pl.when((a + way >= 0) & (a + way < count))
+        def _():
+            pl.semaphore_signal(
+                barrier, inc=1, device_id={"ctx": (a + way) * 4 + b * 2 + c}, device_id_type=MESH
+            )
+
+    for peer in (x_peer, c_peer):
+        pl.semaphore_signal(barrier, inc=1, device_id={"ctx": peer}, device_id_type=MESH)
+    for peer in h_peers.values():
+        pl.semaphore_signal(barrier, inc=1, device_id={"head": peer}, device_id_type=MESH)
+    inner = jnp.where((a > 0) & (a < count - 1), 1, 0)
+    pl.semaphore_wait(barrier, 3 + len(h_peers) + inner)
 
     def copy(src, dst, send, recv, where):
         return pltpu.make_async_remote_copy(
@@ -203,74 +212,144 @@
             device_id=where, device_id_type=MESH,
         )
 
-    sent = []
-
-    def send(*args):
-        out = copy(*args)
-        out.start()
-        sent.append(out)
-
-    mine = slot(index(0, False, False))
-    keep = pltpu.make_async_copy(block_ref, mine, own_sem.at[0])
+    def along(src, at, way, s):
+        n = (0 if way > 0 else count) + s
+        peer = (a + way) * 4 + b * 2 + c
+        return copy(src, slot(at, False, False), z_send.at[n], z_recv.at[n], {"ctx": peer})
+
+    def across(src, at):
+        return copy(src, slot(at, False, False), x_send.at[at], x_recv.at[at], {"ctx": x_peer})
+
+    def core(src, at, far):
+        n = 2 * at + int(far)
+        return copy(src, slot(at, far, False), c_send.at[n], c_recv.at[n], {"ctx": c_peer})
+
+    def valid(at):
+        return (at >= 0) & (at < count)
+
+    load = pltpu.make_async_copy(weight_ref, weight, own_sem.at[2])
+    load.start()
+    keep = pltpu.make_async_copy(block_ref, slot(a, False, False), own_sem.at[0])
     keep.start()
     keep_mixed = pltpu.make_async_copy(mixed_ref, cols(head), own_sem.at[1])
     keep_mixed.start()
-    send(block_ref, mine, x_send.at[0], x_recv.at[0], {"ctx": x_peer})
-    for o in order:
-        send(block_ref, mine, z_send.at[o], z_recv.at[o], {"ctx": z_peers[o]})
-    for o in range(1, heads):
-        send(mixed_ref, cols(head), h_send.at[o], h_recv.at[o], {"head": h_peers[o]})
-    send(block_ref, mine, c_send.at[0], c_recv.at[0], {"ctx": c_peer})
-
-    def arrived(ref, sem, where):
-        copy(ref, ref, own_sem.at[2], sem, where).wait_recv()
-
-    def over_x(o):
-        got = slot(index(o, True, False))
-        arrived(got, x_recv.at[o], {"ctx": x_peer})
-        at = 2 * o + 1
-        send(got, got, c_send.at[at], c_recv.at[at], {"ctx": c_peer})
-
-    before = 0
-    for o in order:
-        got = slot(index(o, False, False))
-        arrived(got, z_recv.at[o], {"ctx": z_peers[o]})
-        send(got, got, x_send.at[o], x_recv.at[o], {"ctx": x_peer})
-        send(got, got, c_send.at[2 * o], c_recv.at[2 * o], {"ctx": c_peer})
-        over_x(before)
-        before = o
-    over_x(before)
-    for o in range(count):
+    across(block_ref, a).start()
+    for way in (1, -1):
+
+        @pl.when(valid(a + way))
+        def _():
+            along(block_ref, a, way, 0).start()
+
+    to_head = {
+        o: copy(mixed_ref, cols(head), h_send.at[o], h_recv.at[o], {"head": h_peers[o]})
+        for o in h_peers
+    }
+    for out in to_head.values():
+        out.start()
+    core(block_ref, a, False).start()
+
+    def over_x(at):
+        got = slot(at, True, False)
+        copy(got, got, x_send.at[at], x_recv.at[at], {"ctx": x_peer}).wait_recv()
+        core(got, at, True).start()
+
+    def over_x_of(s):
+        for way in (1, -1):
+
+            @pl.when(valid(a - way * s))
+            def _():
+                over_x(a - way * s)
+
+    tile = 2 * BLK if weight.shape[0] % (2 * BLK) == 0 else BLK
+    tiles = weight.shape[0] // tile
+    edges = [tiles * t // (count - 1) for t in range(count)]
+
+    def project(t, _):
+        at = pl.multiple_of(t * tile, tile)
+        made = lax.dot_general(
+            wide[...], weight[pl.ds(at, tile), :], NT, preferred_element_type=F32
+        )
+        do_ref[:, pl.ds(at, tile)] = made.astype(BF16)
+        return 0
+
+    for s in range(1, count):
+        for way in (1, -1):
+            at = a - way * s
+
+            @pl.when(valid(at))
+            def _():
+                got = slot(at, False, False)
+                n = (0 if way > 0 else count) + s - 1
+                peer = {"ctx": (a - way) * 4 + b * 2 + c}
+                copy(got, got, z_send.at[n], z_recv.at[n], peer).wait_recv()
+
+                @pl.when(valid(a + way))
+                def _():
+                    along(got, at, way, s).start()
+
+                across(got, at).start()
+                core(got, at, False).start()
+
+        if s == 1:
+            over_x(a)
+        else:
+            over_x_of(s - 1)
+        if s == min(2, count - 1):
+            keep_mixed.wait()
+            load.wait()
+            for o in h_peers:
+                to = cols(lax.rem(head - o + heads, heads))
+                copy(to, to, h_send.at[o], h_recv.at[o], {"head": h_peers[o]}).wait_recv()
+            lax.fori_loop(0, edges[s], project, 0)
+        elif s > 2:
+            lax.fori_loop(edges[s - 1], edges[s], project, 0)
+    over_x_of(count - 1)
+    for at in range(count):
         for far in (False, True):
-            at = 2 * o + int(far)
-            arrived(slot(index(o, far, True)), c_recv.at[at], {"ctx": c_peer})
-    for o in range(1, heads):
-        arrived(cols(lax.rem(head - o + heads, heads)), h_recv.at[o], {"head": h_peers[o]})
-    for out in sent:
+            n = 2 * at + int(far)
+            got = slot(at, far, True)
+            copy(got, got, c_send.at[n], c_recv.at[n], {"ctx": c_peer}).wait_recv()
+    keep.wait()
+    for out in to_head.values():
         out.wait_send()
-    keep.wait()
-    keep_mixed.wait()
-
-
-def gather(block, d_mixed, devices, heads):
+    for way in (1, -1):
+        for s in range(count - 1):
+
+            @pl.when(valid(a - way * s) & valid(a + way))
+            def _():
+                at = a - way * s
+                along(slot(at, False, False), at, way, s).wait_send()
+
+    for at in range(count):
+        across(slot(at, False, False), at).wait_send()
+        for far in (False, True):
+            core(slot(at, far, False), at, far).wait_send()
+
+
+def gather(block, d_mixed, weight, devices, heads):
     count = devices // 4
     dma = pltpu.SemaphoreType.DMA
     hbm = pl.BlockSpec(memory_space=pl.ANY)
+    tokens = d_mixed.shape[0]
     return pl.pallas_call(
         functools.partial(gather_kernel, devices, heads),
         out_shape=(
             jax.ShapeDtypeStruct((devices * block.shape[0], block.shape[1]), BF16),
-            jax.ShapeDtypeStruct((d_mixed.shape[0], heads * d_mixed.shape[1]), BF16),
+            jax.ShapeDtypeStruct((tokens, weight.shape[0]), BF16),
         ),
-        in_specs=[hbm, hbm],
-        out_specs=(hbm, hbm),
+        in_specs=[hbm, hbm, hbm],
+        out_specs=(hbm, pl.BlockSpec(memory_space=pltpu.VMEM)),
         scratch_shapes=[
-            dma((count,)), dma((count,)), dma((count,)), dma((count,)),
+            pltpu.VMEM((tokens, heads * d_mixed.shape[1]), BF16),
+            pltpu.VMEM(weight.shape, BF16),
+            dma((2 * count,)), dma((2 * count,)), dma((count,)), dma((count,)),
             dma((2 * count,)), dma((2 * count,)), dma((heads,)), dma((heads,)), dma((3,)),
         ],
-        compiler_params=pltpu.CompilerParams(collective_id=0, has_side_effects=True),
+        compiler_params=pltpu.CompilerParams(
+            collective_id=0, has_side_effects=True, vmem_limit_bytes=48 * 2**20
+        ),
         name="gather",
-    )(block, d_mixed)
+    )(block, d_mixed, weight)
 
 
 def scatter_kernel(
@@ -382,13 +461,7 @@
         ],
         axis=0,
     )
-    kv_all, mixed = gather(block, d_mixed, devices, split)
-    d_out = lax.dot_general(
-        mixed,
-        out_weight,
-        NT,
-        preferred_element_type=F32,
-    ).astype(BF16)
+    kv_all, d_out = gather(block, d_mixed, out_weight, devices, split)
     own = scope_ids.astype(F32).reshape(tokens // BLK, BLK)
     grad_q, part = attend(
         block_keys, query.reshape(tokens, -1), d_out, kv_all, own, devices, kv

time: 222 us -> 197 us (0.89)
  Pallas kernels: 195 us -> 182 us
  matrix products: 11.9 us -> 0 us
    dot_general x1 -> x0, matrix products: 11.9 us -> none  [on_device(): lax.dot_general(mixed, out_weight, NT, preferred_element_type=F32)]
    pallas_call x1, Pallas kernels: 70.1 us -> 58.4 us  [gather(): pl.pallas_call(functools.partial(gather_kernel, devices, heads), out_shap...]
    unnamed x6 -> x10, local copies, waits for them, and re-layouts: 7.06 us -> 8.04 us
where the time goes in v3:
time: 197 us
  Pallas kernels  182 us (92%)
  local copies, waits for them, and re-layouts  10.7 us (5%)
  other arithmetic  3.27 us (2%)
    pallas_call x1, Pallas kernels, scatter(): pl.pallas_call(functools.partial(scatter_kernel, devices), out_shape=jax....  62.4 us
    pallas_call x1, Pallas kernels, attend(): pl.pallas_call(functools.partial(attend_kernel, devices, tokens, kv, grou...  61.2 us
    pallas_call x1, Pallas kernels, gather(): pl.pallas_call(functools.partial(gather_kernel, devices, heads), out_shap...  58.4 us
    unnamed x10, local copies, waits for them, and re-layouts  8.04 us

profile of v3, /device:TPU:0, one launch (start us, length us, event | category | flops | bytes accessed | tf_op | source)
XLA Modules:
  0.0 196.6 jit_solution(15936819005660760824)
XLA Ops:
  0.6 0.0 copy-start.3
  0.6 0.6 compare_reduce_fusion
  1.3 1.3 broadcast_select_fusion
  2.6 1.2 convert_bitcast_fusion.own_ref
  3.9 1.1 copy_bitcast_fusion.1
  5.0 0.1 pad_maximum_fusion.block_ref
  5.0 0.0 copy-done.3
  5.0 0.0 copy-start.1
  5.1 1.2 copy.17
  6.3 0.0 copy-done.1
  6.3 58.4 %gather.1 = (bf16[4352,1024]{1,0:T(8,128)(2,1)}, bf16[256,2048]{1,0:T(8,128)(2,1)S(1)}) custom-call(bf16[272,1024]{1,0:T(8,128)(2,1)S(1)} %pad_maximum_fusion.block_ref, bf16[256,2048]{1,0:T(8,128)(2,1)S(1)} %copy-done.1, bf16[2048,4096]{1,0:T(8,128)(2,1)} %weight_ref.1), custom_call_target="tpu_custom_call" | custom-call | tf_op jit(solution)/shard_map/gather/pallas_call | solution.py:334
  64.7 0.0 copy-start.2
  64.7 1.0 copy-done.2
  65.7 61.2 %attend.1 = (bf16[256,2048]{1,0:T(8,128)(2,1)}, bf16[4096,1024]{1,0:T(8,128)(2,1)}) custom-call(s32[2,20]{1,0:T(2,128)} %listed.1, bf16[256,2048]{1,0:T(8,128)(2,1)} %bitcast.14, bf16[256,2048]{1,0:T(8,128)(2,1)} %copy-done.2, bf16[4352,1024]{1,0:T(8,128)(2,1)} %get-tuple-element.20.kv_ref, f32[2,128]{1,0:T(2,128)} %convert_bitcast_fusion.own_ref), custom_call_target="tpu_custom_call" | custom-call | tf_op jit(solution)/shard_map/attend/pallas_call | solution.py:133
  126.8 2.4 %copy.13 = bf16[32,8,16,128]{3,2,1,0:T(8,128)(2,1)} copy(bf16[32,8,16,128]{3,1,2,0:T(8,128)(2,1)} %bitcast.17) | data formatting | bytes 2097152
  129.3 0.0 copy-start
  129.3 3.4 %copy-done = bf16[4096,1024]{1,0:T(8,128)(2,1)S(1)} copy-done((bf16[4096,1024]{1,0:T(8,128)(2,1)S(1)}, bf16[4096,1024]{1,0:T(8,128)(2,1)}, u32[]{:S(2)}) %copy-start) | copy-done | bytes 8388632
  132.6 62.4 %scatter.10 = bf16[256,1024]{1,0:T(8,128)(2,1)S(1)} custom-call(bf16[4096,1024]{1,0:T(8,128)(2,1)S(1)} %copy-done), custom_call_target="tpu_custom_call" | custom-call | tf_op jit(solution)/shard_map/scatter/pallas_call | solution.py:431
  195.1 0.8 reshape.58
  195.8 0.8 reshape.57
  (3 shorter events, 0.0 us)
Async XLA Ops:
  0.6 4.4 %copy-start.3 = (bf16[256,16,128]{2,1,0:T(8,128)(2,1)S(1)}, bf16[256,16,128]{2,1,0:T(8,128)(2,1)}, u32[]{:S(2)}) copy-start(bf16[256,16,128]{2,1,0:T(8,128)(2,1)} %param.9) | copy-start | bytes 3145732
  5.0 1.3 copy-start.1
  64.7 1.0 copy-start.2
  129.3 3.4 %copy-start = (bf16[4096,1024]{1,0:T(8,128)(2,1)S(1)}, bf16[4096,1024]{1,0:T(8,128)(2,1)}, u32[]{:S(2)}) copy-start(bf16[4096,1024]{1,0:T(8,128)(2,1)} %get-tuple-element.22.part_ref) | copy-start | bytes 25165828

commit v4 on v3

--- a/solution.py
+++ b/solution.py
@@ -24,7 +24,7 @@
     blocks = tokens // BLK
     width = BLK
     wide = group * BLK
-    cut = next(c for c in (4, 2, 1) if slots % c == 0)
+    cut = next(c for c in (10, 5, 4, 2, 1) if slots % c == 0)
     chunk = cut * BLK
     scale = 1.0 / math.sqrt(width)
     log2e = scale * math.log2(math.e)

time: 197 us -> 188 us (0.954)
  Pallas kernels: 182 us -> 172 us
    pallas_call x1, Pallas kernels: 61.2 us -> 51.7 us  [attend(): pl.pallas_call(functools.partial(attend_kernel, devices, tokens, kv, grou...]
where the time goes in v4:
time: 188 us; the launch traced here: 187 us
  Pallas kernels  172 us (91%)
  local copies, waits for them, and re-layouts  10.7 us (6%)
  other arithmetic  3.27 us (2%)
    pallas_call x1, Pallas kernels, scatter(): pl.pallas_call(functools.partial(scatter_kernel, devices), out_shape=jax....  62.4 us
    pallas_call x1, Pallas kernels, gather(): pl.pallas_call(functools.partial(gather_kernel, devices, heads), out_shap...  58.4 us
    pallas_call x1, Pallas kernels, attend(): pl.pallas_call(functools.partial(attend_kernel, devices, tokens, kv, grou...  51.7 us
    unnamed x10, local copies, waits for them, and re-layouts  8.04 us

profile of v4, /device:TPU:0, one launch (start us, length us, event | category | flops | bytes accessed | tf_op | source)
XLA Modules:
  0.0 187.1 jit_solution(5472508813166053569)
XLA Ops:
  0.6 0.0 copy-start.3
  0.6 0.6 compare_reduce_fusion
  1.3 1.3 broadcast_select_fusion
  2.6 1.2 convert_bitcast_fusion.own_ref
  3.9 1.1 copy_bitcast_fusion.1
  5.0 0.1 pad_maximum_fusion.block_ref
  5.0 0.0 copy-done.3
  5.0 0.0 copy-start.1
  5.1 1.2 copy.17
  6.3 0.0 copy-done.1
  6.3 58.4 %gather.1 = (bf16[4352,1024]{1,0:T(8,128)(2,1)}, bf16[256,2048]{1,0:T(8,128)(2,1)S(1)}) custom-call(bf16[272,1024]{1,0:T(8,128)(2,1)S(1)} %pad_maximum_fusion.block_ref, bf16[256,2048]{1,0:T(8,128)(2,1)S(1)} %copy-done.1, bf16[2048,4096]{1,0:T(8,128)(2,1)} %weight_ref.1), custom_call_target="tpu_custom_call" | custom-call | tf_op jit(solution)/shard_map/gather/pallas_call | solution.py:334
  64.7 0.0 copy-start.2
  64.7 1.0 copy-done.2
  65.7 51.7 %attend.1 = (bf16[256,2048]{1,0:T(8,128)(2,1)}, bf16[4096,1024]{1,0:T(8,128)(2,1)}) custom-call(s32[2,20]{1,0:T(2,128)} %listed.1, bf16[256,2048]{1,0:T(8,128)(2,1)} %bitcast.14, bf16[256,2048]{1,0:T(8,128)(2,1)} %copy-done.2, bf16[4352,1024]{1,0:T(8,128)(2,1)} %get-tuple-element.20.kv_ref, f32[2,128]{1,0:T(2,128)} %convert_bitcast_fusion.own_ref), custom_call_target="tpu_custom_call" | custom-call | tf_op jit(solution)/shard_map/attend/pallas_call | solution.py:133
  117.4 2.4 %copy.13 = bf16[32,8,16,128]{3,2,1,0:T(8,128)(2,1)} copy(bf16[32,8,16,128]{3,1,2,0:T(8,128)(2,1)} %bitcast.17) | data formatting | bytes 2097152
  119.8 0.0 copy-start
  119.8 3.4 %copy-done = bf16[4096,1024]{1,0:T(8,128)(2,1)S(1)} copy-done((bf16[4096,1024]{1,0:T(8,128)(2,1)S(1)}, bf16[4096,1024]{1,0:T(8,128)(2,1)}, u32[]{:S(2)}) %copy-start) | copy-done | bytes 8388632
  123.2 62.4 %scatter.10 = bf16[256,1024]{1,0:T(8,128)(2,1)S(1)} custom-call(bf16[4096,1024]{1,0:T(8,128)(2,1)S(1)} %copy-done), custom_call_target="tpu_custom_call" | custom-call | tf_op jit(solution)/shard_map/scatter/pallas_call | solution.py:431
  185.6 0.8 reshape.58
  186.4 0.8 reshape.57
  (3 shorter events, 0.0 us)
Async XLA Ops:
  0.6 4.4 %copy-start.3 = (bf16[256,16,128]{2,1,0:T(8,128)(2,1)S(1)}, bf16[256,16,128]{2,1,0:T(8,128)(2,1)}, u32[]{:S(2)}) copy-start(bf16[256,16,128]{2,1,0:T(8,128)(2,1)} %param.9) | copy-start | bytes 3145732
  5.0 1.3 copy-start.1
  64.7 1.0 copy-start.2
  119.8 3.4 %copy-start = (bf16[4096,1024]{1,0:T(8,128)(2,1)S(1)}, bf16[4096,1024]{1,0:T(8,128)(2,1)}, u32[]{:S(2)}) copy-start(bf16[4096,1024]{1,0:T(8,128)(2,1)} %get-tuple-element.22.part_ref) | copy-start | bytes 25165828
